TPU v7x, 32 devices: a whole 2x2x4 slice. The times are simulated.
32 devices in a mesh: cells: 8 (over z, y), dirs: 4 (over x, core).
Axes of the slice: x: 2, y: 2, z: 4, core: 2. Of those that a mesh axis runs over, the one named last changes fastest.
Arguments:
- incident: float32 [512, 6144], P('cells', 'dirs'), may hold values from -24 to 24
- scattering: float32 [512, 192], P('cells'), may hold values from 0.1 to 1
- translations: bfloat16 [8, 192, 192], replicated, may hold values from -1.5 to 1.5
- pair_sphere: int32 [512, 16], P('cells'), may hold values from 0 to 511, as said below
- pair_class: int32 [512, 16], P('cells'), may hold values from 0 to 7
- pair_weight: bfloat16 [512, 16], P('cells'), may hold values from 0.19921875 to 0.796875
- pair_mask: int32 [512, 16], P('cells'), may hold values from 0 to 1, as said below
Outputs:
- solution: float32 [512, 6144], P('cells', 'dirs')
- residual: float32 [512, 6144], P('cells', 'dirs')
- dual_residual: float32 [512, 6144], P('cells', 'dirs')
- direction: float32 [512, 6144], P('cells', 'dirs')
Inputs may be any that keep to these rules, and one draw needn't show every extreme that they name: `pair_sphere`: sphere ids are cell-major: cell c holds spheres 64 c to 64 (c + 1) - 1, and the cells form a cycle. The slots of one sphere name distinct spheres, never the sphere itself; each named sphere lies in the sphere's own cell, or among the last 32 spheres of the previous cell, or among the first 32 spheres of the next cell. In every cell the first sphere names sphere 64 - 32 of the previous cell and the last sphere names sphere 32 - 1 of the next, both in live slots. `pair_mask`: the live slots of a sphere come first; the first and the last sphere of every cell have all 16 slots live, every sphere at least 8.
All inputs are finite; a program needn't handle non-finite values.
Results may differ from a plain program's by a relative error of at most 0.0003.
The roundings to bfloat16 on the way count: a program that leaves them out, or rounds other values in their place, can miss the bound.
Values may be sent and summed in bfloat16 or wider, within the bound.
A program may use at most 64 MiB of HBM per device.

v0:
```python
import jax
import jax.numpy as jnp
from jax import lax
from jax.sharding import PartitionSpec as P


def extended(x, sides, width):
    for axis, dim in sides:
        devices, length = (lax.axis_size(axis), x.shape[dim])
        up = [(i, (i + 1) % devices) for i in range(devices)]
        down = [(j, i) for i, j in up]
        last = lax.slice_in_dim(x, length - width, length, axis=dim)
        leading = lax.slice_in_dim(x, 0, width, axis=dim)
        before = lax.ppermute(last, axis, up)
        after = lax.ppermute(leading, axis, down)
        x = jnp.concatenate([before, x, after], axis=dim)
    return x


def passed_along(x, axis, by):
    devices = lax.axis_size(axis)
    return lax.ppermute(x, axis, [(i, (i + by) % devices) for i in range(devices)])


def on_device(incident, scattering, translations, pair_sphere, pair_class, pair_weight, pair_mask):
    spheres = incident.shape[0]
    columns = incident.shape[1]
    order = translations.shape[1]
    groups = columns // order
    classes = translations.shape[0]
    extent = spheres + 2 * spheres
    source = incident.astype(jnp.bfloat16)
    padded = extended(source, (("cells", 0),), spheres)
    position = lax.axis_index("cells")
    cell_count = lax.axis_size("cells")
    owner = pair_sphere // spheres
    within = pair_sphere % spheres
    offset = (owner - position) % cell_count
    column = jnp.where(
        offset == 0,
        spheres + within,
        jnp.where(offset == 1, spheres + spheres + within, spheres - spheres + within),
    )
    placed = (column[:, :, None] == jnp.arange(extent, dtype=jnp.int32)[None, None, :]).astype(
        jnp.bfloat16
    )
    strength = pair_weight.astype(jnp.float32) * pair_mask.astype(jnp.float32)
    chosen = pair_class[:, :, None] == jnp.arange(classes, dtype=jnp.int32)[None, None, :]
    coupling = jnp.where(chosen, strength[:, :, None], jnp.float32(0.0)).astype(jnp.bfloat16)
    blocks = jnp.einsum("smk,smc->ksc", coupling, placed, preferred_element_type=jnp.float32)
    blocks_half = blocks.astype(jnp.bfloat16)

    def primal_step(total, pieces):
        block, operator = pieces
        summed = jnp.dot(block, padded, preferred_element_type=jnp.float32).astype(jnp.bfloat16)
        moved = jnp.dot(
            summed.reshape(spheres * groups, order), operator, preferred_element_type=jnp.float32
        )
        return (total + moved.reshape(spheres, columns), None)

    coupled, unused = lax.scan(
        primal_step, jnp.zeros((spheres, columns), jnp.float32), (blocks_half, translations)
    )
    gain = jnp.tile(scattering, (1, groups))
    image = incident - gain * coupled
    weighted = (gain * incident).astype(jnp.bfloat16)
    flat_weighted = weighted.reshape(spheres * groups, order)

    def dual_step(total, pieces):
        block, operator = pieces
        moved = lax.dot_general(
            flat_weighted, operator, (((1,), (1,)), ((), ())), preferred_element_type=jnp.float32
        )
        spread = lax.dot_general(
            block,
            moved.reshape(spheres, columns),
            (((0,), (0,)), ((), ())),
            precision=lax.Precision.HIGHEST,
            preferred_element_type=jnp.float32,
        )
        return (total + spread, None)

    contrib, unused_two = lax.scan(
        dual_step, jnp.zeros((extent, columns), jnp.float32), (blocks, translations)
    )
    lower_part = contrib[:spheres]
    upper_part = contrib[spheres + spheres :]
    from_next = passed_along(lower_part, "cells", -1)
    from_prev = passed_along(upper_part, "cells", 1)
    back = contrib[spheres : spheres + spheres]
    back = back.at[spheres - spheres :].add(from_next)
    back = back.at[:spheres].add(from_prev)
    dual_image = incident - back
    norm_old, along_image, along_dual, cross_term = lax.psum(
        (
            jnp.sum(incident * incident),
            jnp.sum(incident * image),
            jnp.sum(dual_image * incident),
            jnp.sum(dual_image * image),
        ),
        ("cells", "dirs"),
    )
    step_size = norm_old / along_image
    solution = step_size * incident
    residual = incident - step_size * image
    dual_residual = incident - step_size * dual_image
    norm_new = (
        norm_old - step_size * (along_image + along_dual) + step_size * step_size * cross_term
    )
    direction = residual + norm_new / norm_old * incident
    return (solution, residual, dual_residual, direction)


def solution(mesh):
    placed = (
        P("cells", "dirs"),
        P("cells", None),
        P(),
        P("cells", None),
        P("cells", None),
        P("cells", None),
        P("cells", None),
    )
    return jax.shard_map(
        on_device,
        mesh=mesh,
        in_specs=placed,
        out_specs=(P("cells", "dirs"), P("cells", "dirs"), P("cells", "dirs"), P("cells", "dirs")),
        check_vma=False,
    )
```

profile of v0, /device:TPU:0, one launch (start us, length us, event | category | flops | bytes accessed | tf_op | source)
XLA Modules:
  0.0 115.8 jit_solution(3186098744896755521)
XLA Ops:
  1.9 6.1 %collective-permute-start.1 = (bf16[64,1536]{1,0:T(8,128)(2,1)S(1)}, bf16[64,1536]{1,0:T(8,128)(2,1)S(1)}, u32[]{:S(2)}, u32[]{:S(2)}) collective-permute-start(bf16[64,1536]{1,0:T(8,128)(2,1)S(1)} %get-tuple-element.192), channel_id=1, source_target_pairs={{4,0},{8,4},{12,8},{16,12},{20,16},{24,20},{28,24},{0,28},{5,1},{9... | collective-permute-start | bytes 589832 | tf_op jit(solution)/shard_map/ppermute | solution.py:15
  9.1 29.6 %while.27 = (s32[]{:T(128)}, f32[192,1536]{1,0:T(8,128)S(1)}, f32[8,64,192]{2,0,1:T(8,128)S(1)}, bf16[8,192,192]{2,1,0:T(8,128)(2,1)}, bf16[512,192]{1,0:T(8,128)(2,1)S(1)}, /*index=5*/s32[]{:T(128)}, s32[]{:T(128)}) while((s32[]{:T(128)}, f32[192,1536]{1,0:T(8,128)S(1)}, f32[8,64,192]{2,0,1:T(8,128)S(1)}, ...), condition=%wide.region_7.8_spmd.clone, body=%wide.region_6.7_spmd.clone.sunk | while | flops 264830976 | bytes 8306847 | solution.py:83
  9.9 1.1 convolution_bitcast_fusion.3
  11.4 1.3 %convolution_add_fusion.2 = f32[192,1536]{1,0:T(8,128)S(1)} fusion(f32[64,1536]{1,0:T(8,128)S(1)} %reshape.86, f32[192,1536]{1,0:T(8,128)S(1)} %get-tuple-element.286, pred[]{:T(512)S(6)} %compare.27, f32[1,64,192]{2,0,1:T(1,128)S(1)} %constant_dynamic-slice_fusion.2), kind=kOutput, calls=%fused_computation.9.clone.1 | convolution fusion | flops 227082240 | bytes 2801665 | tf_op jit(solution)/shard_map/while/body/eval_jaxpr/dot_general | solution.py:74
  13.6 1.1 convolution_bitcast_fusion.3
  15.1 1.3 %convolution_add_fusion.2 = f32[192,1536]{1,0:T(8,128)S(1)} fusion(f32[64,1536]{1,0:T(8,128)S(1)} %reshape.86, f32[192,1536]{1,0:T(8,128)S(1)} %get-tuple-element.286, pred[]{:T(512)S(6)} %compare.27, f32[1,64,192]{2,0,1:T(1,128)S(1)} %constant_dynamic-slice_fusion.2), kind=kOutput, calls=%fused_computation.9.clone.1 | convolution fusion | flops 227082240 | bytes 2801665 | tf_op jit(solution)/shard_map/while/body/eval_jaxpr/dot_general | solution.py:74
  17.3 1.1 convolution_bitcast_fusion.3
  18.8 1.3 %convolution_add_fusion.2 = f32[192,1536]{1,0:T(8,128)S(1)} fusion(f32[64,1536]{1,0:T(8,128)S(1)} %reshape.86, f32[192,1536]{1,0:T(8,128)S(1)} %get-tuple-element.286, pred[]{:T(512)S(6)} %compare.27, f32[1,64,192]{2,0,1:T(1,128)S(1)} %constant_dynamic-slice_fusion.2), kind=kOutput, calls=%fused_computation.9.clone.1 | convolution fusion | flops 227082240 | bytes 2801665 | tf_op jit(solution)/shard_map/while/body/eval_jaxpr/dot_general | solution.py:74
  21.0 1.1 convolution_bitcast_fusion.3
  22.5 1.3 %convolution_add_fusion.2 = f32[192,1536]{1,0:T(8,128)S(1)} fusion(f32[64,1536]{1,0:T(8,128)S(1)} %reshape.86, f32[192,1536]{1,0:T(8,128)S(1)} %get-tuple-element.286, pred[]{:T(512)S(6)} %compare.27, f32[1,64,192]{2,0,1:T(1,128)S(1)} %constant_dynamic-slice_fusion.2), kind=kOutput, calls=%fused_computation.9.clone.1 | convolution fusion | flops 227082240 | bytes 2801665 | tf_op jit(solution)/shard_map/while/body/eval_jaxpr/dot_general | solution.py:74
  24.6 1.1 convolution_bitcast_fusion.3
  26.2 1.3 %convolution_add_fusion.2 = f32[192,1536]{1,0:T(8,128)S(1)} fusion(f32[64,1536]{1,0:T(8,128)S(1)} %reshape.86, f32[192,1536]{1,0:T(8,128)S(1)} %get-tuple-element.286, pred[]{:T(512)S(6)} %compare.27, f32[1,64,192]{2,0,1:T(1,128)S(1)} %constant_dynamic-slice_fusion.2), kind=kOutput, calls=%fused_computation.9.clone.1 | convolution fusion | flops 227082240 | bytes 2801665 | tf_op jit(solution)/shard_map/while/body/eval_jaxpr/dot_general | solution.py:74
  28.3 1.1 convolution_bitcast_fusion.3
  29.9 1.3 %convolution_add_fusion.2 = f32[192,1536]{1,0:T(8,128)S(1)} fusion(f32[64,1536]{1,0:T(8,128)S(1)} %reshape.86, f32[192,1536]{1,0:T(8,128)S(1)} %get-tuple-element.286, pred[]{:T(512)S(6)} %compare.27, f32[1,64,192]{2,0,1:T(1,128)S(1)} %constant_dynamic-slice_fusion.2), kind=kOutput, calls=%fused_computation.9.clone.1 | convolution fusion | flops 227082240 | bytes 2801665 | tf_op jit(solution)/shard_map/while/body/eval_jaxpr/dot_general | solution.py:74
  32.0 1.1 convolution_bitcast_fusion.3
  33.6 1.3 %convolution_add_fusion.2 = f32[192,1536]{1,0:T(8,128)S(1)} fusion(f32[64,1536]{1,0:T(8,128)S(1)} %reshape.86, f32[192,1536]{1,0:T(8,128)S(1)} %get-tuple-element.286, pred[]{:T(512)S(6)} %compare.27, f32[1,64,192]{2,0,1:T(1,128)S(1)} %constant_dynamic-slice_fusion.2), kind=kOutput, calls=%fused_computation.9.clone.1 | convolution fusion | flops 227082240 | bytes 2801665 | tf_op jit(solution)/shard_map/while/body/eval_jaxpr/dot_general | solution.py:74
  35.7 1.1 convolution_bitcast_fusion.3
  37.3 1.3 %convolution_add_fusion.2 = f32[192,1536]{1,0:T(8,128)S(1)} fusion(f32[64,1536]{1,0:T(8,128)S(1)} %reshape.86, f32[192,1536]{1,0:T(8,128)S(1)} %get-tuple-element.286, pred[]{:T(512)S(6)} %compare.27, f32[1,64,192]{2,0,1:T(1,128)S(1)} %constant_dynamic-slice_fusion.2), kind=kOutput, calls=%fused_computation.9.clone.1 | convolution fusion | flops 227082240 | bytes 2801665 | tf_op jit(solution)/shard_map/while/body/eval_jaxpr/dot_general | solution.py:74
  39.6 4.7 %collective-permute-start.2 = (f32[64,1536]{1,0:T(8,128)}, f32[64,1536]{1,0:T(8,128)}, u32[]{:S(2)}, u32[]{:S(2)}) collective-permute-start(f32[64,1536]{1,0:T(8,128)} %get-tuple-element.187), channel_id=1, source_target_pairs={{0,28},{4,0},{8,4},{12,8},{16,12},{20,16},{24,20},{28,24},{1,29},{... | collective-permute-start | bytes 1179656 | tf_op jit(solution)/shard_map/ppermute | solution.py:22
  46.0 21.3 %while.26 = (s32[]{:T(128)}, f32[64,1536]{1,0:T(8,128)S(1)}, bf16[8,64,192]{2,1,0:T(8,128)(2,1)}, bf16[192,1536]{1,0:T(8,128)(2,1)S(1)}, bf16[8,192,192]{2,1,0:T(8,128)(2,1)}, /*index=5*/s32[]{:T(128)}, s32[]{:T(128)}) while((s32[]{:T(128)}, f32[64,1536]{1,0:T(8,128)S(1)}, bf16[8,64,192]{2,1,0:T(8,128)(2,1)}, ...), condition=%wide.region_3.4_spmd.clone, body=%wide.region_2.3_spmd.clone.sunk | while | flops 75792384 | bytes 3866727 | solution.py:61
  47.3 1.1 fusion.37
  49.9 1.1 fusion.37
  52.6 1.1 fusion.37
  54.0 1.0 convolution_convert_fusion.2
  55.2 1.1 fusion.37
  57.9 1.1 fusion.37
  60.6 1.1 fusion.37
  63.2 1.1 fusion.37
  65.9 1.1 fusion.37
  67.4 2.1 %multiply_reduce_fusion = (f32[]{:T(128)}, f32[]{:T(128)}, f32[]{:T(128)}, f32[]{:T(128)}, f32[64,1536]{1,0:T(8,128)S(1)}) fusion(f32[64,1536]{1,0:T(8,128)} %param.19, f32[64,1536]{1,0:T(8,128)S(1)} %tile.10, f32[64,1536]{1,0:T(8,128)S(1)} %get-tuple-element.98, f32[64,1536]{1,0:T(8,128)} %collective-permute-done.3, f32[64,1536]{1,0:T(8,128)} %collective-permute-done.2, ...), kind=kLoop, calls=%fused_computation.21 | loop fusion | flops 1277948 | bytes 2752528 | tf_op jit(solution)/shard_map/reduce_sum | solution.py:99
  69.5 40.4 %all-reduce = (f32[]{:T(128)}, f32[]{:T(128)}, f32[]{:T(128)}, f32[]{:T(128)}) all-reduce(f32[]{:T(128)} %get-tuple-element.159, f32[]{:T(128)} %get-tuple-element.157, f32[]{:T(128)} %get-tuple-element.158, f32[]{:T(128)} %get-tuple-element.156), channel_id=1, replica_groups=mesh['cells'=8,'dirs'=4] {'cells','dirs'}, use_global_device_ids=true, to_apply=%region_1.2 | all-reduce | flops 4 | bytes 32 | tf_op jit(solution)/shard_map/psum | solution.py:94
  114.5 1.2 %multiply_add_fusion = (f32[64,1536]{1,0:T(8,128)}, f32[64,1536]{1,0:T(8,128)}, f32[64,1536]{1,0:T(8,128)}, f32[64,1536]{1,0:T(8,128)}) fusion(f32[64,1536]{1,0:T(8,128)S(1)} %copy-done.1, f32[]{:T(128)S(6)} %div.23, f32[64,1536]{1,0:T(8,128)S(1)} %tile.10, f32[64,1536]{1,0:T(8,128)S(1)} %get-tuple-element.98, f32[]{:T(128)S(6)} %div.22, ...), kind=kLoop, calls=%fused_computation.20 | loop fusion | flops 884736 | bytes 3145736 | tf_op jit(solution)/shard_map/add | solution.py:110
  (120 shorter events, 25.1 us)
Async XLA Ops:
  0.6 1.2 %copy-start = (f32[64,1536]{1,0:T(8,128)S(1)}, f32[64,1536]{1,0:T(8,128)}, u32[]{:S(2)}) copy-start(f32[64,1536]{1,0:T(8,128)} %param.19) | copy-start | bytes 1179652
  1.6 6.4 %copy-start.5 = (s32[64,16]{0,1:T(8,128)S(1)}, s32[64,16]{0,1:T(8,128)}, u32[]{:S(2)}) copy-start(s32[64,16]{0,1:T(8,128)} %param.25) | copy-start | bytes 12292
  1.6 6.3 %copy-start.7 = (bf16[64,16]{0,1:T(8,128)(2,1)S(1)}, bf16[64,16]{0,1:T(8,128)(2,1)}, u32[]{:S(2)}) copy-start(bf16[64,16]{0,1:T(8,128)(2,1)} %param.24) | copy-start | bytes 6148
  1.6 6.5 %copy-start.6 = (s32[64,16]{0,1:T(8,128)S(1)}, s32[64,16]{0,1:T(8,128)}, u32[]{:S(2)}) copy-start(s32[64,16]{0,1:T(8,128)} %param.22) | copy-start | bytes 12292
  1.6 6.6 %copy-start.4 = (s32[64,16]{0,1:T(8,128)S(1)}, s32[64,16]{0,1:T(8,128)}, u32[]{:S(2)}) copy-start(s32[64,16]{0,1:T(8,128)} %param.23) | copy-start | bytes 12292
  1.9 43.2 %collective-permute-start.1 = (bf16[64,1536]{1,0:T(8,128)(2,1)S(1)}, bf16[64,1536]{1,0:T(8,128)(2,1)S(1)}, u32[]{:S(2)}, u32[]{:S(2)}) collective-permute-start(bf16[64,1536]{1,0:T(8,128)(2,1)S(1)} %get-tuple-element.192), channel_id=1, source_target_pairs={{4,0},{8,4},{12,8},{16,12},{20,16},{24,20},{28,24},{0,28},{5,1},{9... | collective-permute-start | bytes 589832 | tf_op jit(solution)/shard_map/ppermute | solution.py:15
  7.9 37.1 %collective-permute-start = (bf16[64,1536]{1,0:T(8,128)(2,1)S(1)}, bf16[64,1536]{1,0:T(8,128)(2,1)}, u32[]{:S(2)}, u32[]{:S(2)}) collective-permute-start(bf16[64,1536]{1,0:T(8,128)(2,1)S(1)} %get-tuple-element.192), channel_id=1, source_target_pairs={{0,4},{4,8},{8,12},{12,16},{16,20},{20,24},{24,28},{28,0},{1,5},{5... | collective-permute-start | bytes 589832 | tf_op jit(solution)/shard_map/ppermute | solution.py:14
  9.1 0.8 copy-start.2
  11.4 1.4 %copy-start.3 = (f32[8,64,192]{2,0,1:T(8,128)S(1)}, f32[8,64,192]{2,0,1:T(8,128)}, u32[]{:S(2)}) copy-start(f32[8,64,192]{2,0,1:T(8,128)} %copy-done.2) | copy-start | bytes 1179652 | tf_op jit(solution)/shard_map/while
  12.8 0.8 copy-start.2
  15.1 1.4 %copy-start.3 = (f32[8,64,192]{2,0,1:T(8,128)S(1)}, f32[8,64,192]{2,0,1:T(8,128)}, u32[]{:S(2)}) copy-start(f32[8,64,192]{2,0,1:T(8,128)} %copy-done.2) | copy-start | bytes 1179652 | tf_op jit(solution)/shard_map/while
  16.5 0.8 copy-start.2
  18.8 1.4 %copy-start.3 = (f32[8,64,192]{2,0,1:T(8,128)S(1)}, f32[8,64,192]{2,0,1:T(8,128)}, u32[]{:S(2)}) copy-start(f32[8,64,192]{2,0,1:T(8,128)} %copy-done.2) | copy-start | bytes 1179652 | tf_op jit(solution)/shard_map/while
  20.2 0.8 copy-start.2
  22.5 1.4 %copy-start.3 = (f32[8,64,192]{2,0,1:T(8,128)S(1)}, f32[8,64,192]{2,0,1:T(8,128)}, u32[]{:S(2)}) copy-start(f32[8,64,192]{2,0,1:T(8,128)} %copy-done.2) | copy-start | bytes 1179652 | tf_op jit(solution)/shard_map/while
  23.9 0.8 copy-start.2
  26.2 1.4 %copy-start.3 = (f32[8,64,192]{2,0,1:T(8,128)S(1)}, f32[8,64,192]{2,0,1:T(8,128)}, u32[]{:S(2)}) copy-start(f32[8,64,192]{2,0,1:T(8,128)} %copy-done.2) | copy-start | bytes 1179652 | tf_op jit(solution)/shard_map/while
  27.6 0.8 copy-start.2
  29.9 1.4 %copy-start.3 = (f32[8,64,192]{2,0,1:T(8,128)S(1)}, f32[8,64,192]{2,0,1:T(8,128)}, u32[]{:S(2)}) copy-start(f32[8,64,192]{2,0,1:T(8,128)} %copy-done.2) | copy-start | bytes 1179652 | tf_op jit(solution)/shard_map/while
  31.3 0.8 copy-start.2
  33.6 1.4 %copy-start.3 = (f32[8,64,192]{2,0,1:T(8,128)S(1)}, f32[8,64,192]{2,0,1:T(8,128)}, u32[]{:S(2)}) copy-start(f32[8,64,192]{2,0,1:T(8,128)} %copy-done.2) | copy-start | bytes 1179652 | tf_op jit(solution)/shard_map/while
  35.0 0.8 copy-start.2
  37.3 1.4 %copy-start.3 = (f32[8,64,192]{2,0,1:T(8,128)S(1)}, f32[8,64,192]{2,0,1:T(8,128)}, u32[]{:S(2)}) copy-start(f32[8,64,192]{2,0,1:T(8,128)} %copy-done.2) | copy-start | bytes 1179652 | tf_op jit(solution)/shard_map/while
  39.6 27.8 %collective-permute-start.2 = (f32[64,1536]{1,0:T(8,128)}, f32[64,1536]{1,0:T(8,128)}, u32[]{:S(2)}, u32[]{:S(2)}) collective-permute-start(f32[64,1536]{1,0:T(8,128)} %get-tuple-element.187), channel_id=1, source_target_pairs={{0,28},{4,0},{8,4},{12,8},{16,12},{20,16},{24,20},{28,24},{1,29},{... | collective-permute-start | bytes 1179656 | tf_op jit(solution)/shard_map/ppermute | solution.py:22
  44.3 23.1 %collective-permute-start.3 = (f32[64,1536]{1,0:T(8,128)}, f32[64,1536]{1,0:T(8,128)}, u32[]{:S(2)}, u32[]{:S(2)}) collective-permute-start(f32[64,1536]{1,0:T(8,128)} %get-tuple-element.188), channel_id=1, source_target_pairs={{0,4},{4,8},{8,12},{12,16},{16,20},{20,24},{24,28},{28,0},{1,5},{5... | collective-permute-start | bytes 1179656 | tf_op jit(solution)/shard_map/ppermute | solution.py:22
  67.4 47.2 %copy-start.1 = (f32[64,1536]{1,0:T(8,128)S(1)}, f32[64,1536]{1,0:T(8,128)}, u32[]{:S(2)}) copy-start(f32[64,1536]{1,0:T(8,128)} %param.19) | copy-start | bytes 1179652
where the time goes:
time: 117 us; the launch traced here: 116 us
  blocking collectives  40.4 us (35%)
  matrix products  37 us (32%)
  local copies, waits for them, and re-layouts  15.6 us (13%)
  starting transfers between devices  10.8 us (9%)
  between operations  5.4 us (5%)
  other arithmetic  5.37 us (5%)
    psum x1, blocking collectives, on_device(): lax.psum((jnp.sum(incident * incident), jnp.sum(incident * image), jnp.su...  40.4 us
    dot_general x8, matrix products, dual_step(): lax.dot_general(block, moved.reshape(spheres, columns), (((0,), (0,)), ((...  10.7 us
    dot_general x8, matrix products, dual_step(): lax.dot_general(flat_weighted, operator, (((1,), (1,)), ((), ())), prefer...  9.07 us
    dot_general x8, matrix products, primal_step(): jnp.dot(summed.reshape(spheres * groups, order), operator, preferred_elem...  8.84 us
    dot_general x8, matrix products, primal_step(): jnp.dot(block, padded, preferred_element_type=jnp.float32)  7.85 us
    ppermute x1, starting transfers between devices, extended(): after = lax.ppermute(leading, axis, down)  6.06 us
    while x32, local copies, waits for them, and re-layouts  5.76 us
    ppermute x2, starting transfers between devices, passed_along(): lax.ppermute(x, axis, [(i, (i + by) % devices) for i in range(devices)])  4.71 us
  transfers between devices with their start and end apart: 4, of which 0 were waited for; matrix products, arithmetic and copies ran while one was open for 41% of the time, Pallas kernels for 0%

commit v1 on v0

v1 whole, which is shorter than its diff:
```python
import functools
import jax
import jax.numpy as jnp
from jax import lax
from jax.experimental import pallas as pl
from jax.experimental.pallas import tpu as pltpu
from jax.sharding import PartitionSpec as P

F32 = jnp.float32
BF16 = jnp.bfloat16
STRIDE = 256


def folded(x):
    rows, width = x.shape
    y = jnp.sum(x.reshape(rows // 8, 8, width), axis=0)
    out = y[:, :128]
    for at in range(128, width, 128):
        out = out + y[:, at : at + 128]
    return out


def kernel(
    cells,
    dirs,
    inc_ref,
    sc_ref,
    tr_ref,
    ps_ref,
    pc_ref,
    pw_ref,
    pm_ref,
    img_ref,
    dual_ref,
    coef_ref,
    send,
    from_prev,
    from_next,
    meta,
    meta_prev,
    meta_next,
    gain,
    pick,
    dpick,
    te,
    to,
    tet,
    tot,
    gs,
    ghi,
    glo,
    red_d,
    red_c,
    ssem,
    rsem,
    msem,
    mrsem,
    dssem,
    drsem,
    cssem,
    crsem,
):
    rows, columns = inc_ref.shape
    band = rows // 2
    classes, order, _ = tr_ref.shape
    slots = ps_ref.shape[1]
    wide = 2 * order
    pairs = columns // wide
    me = lax.axis_index("cells")
    my_dir = lax.axis_index("dirs")
    right = lax.rem(me + 1, cells)
    left = lax.rem(me + cells - 1, cells)

    barrier = pltpu.get_barrier_semaphore()

    def greet_cell(t, c):
        pl.semaphore_signal(
            barrier, inc=1, device_id=(lax.rem(me + t, cells), my_dir), device_id_type=pl.DeviceIdType.MESH
        )
        return c

    def greet_dir(t, c):
        pl.semaphore_signal(
            barrier, inc=1, device_id=(me, lax.rem(my_dir + t, dirs)), device_id_type=pl.DeviceIdType.MESH
        )
        return c

    lax.fori_loop(1, cells, greet_cell, 0)
    lax.fori_loop(1, dirs, greet_dir, 0)

    gain[:, 0:order] = sc_ref[...]
    gain[:, order:wide] = sc_ref[...]
    g = gain[...]
    for p in range(pairs):
        x = inc_ref[:, p * wide : (p + 1) * wide]
        src = x.astype(BF16)
        send[p, 0:band, :] = src[0:band]
        send[p, band : band + rows, :] = (g * x).astype(BF16)
        send[p, band + rows :, :] = src[band:]

    ps = ps_ref[...]
    owner = ps // rows
    within = ps - owner * rows
    off = owner - me
    is_own = off == 0
    is_next = (off == 1) | (off == 1 - cells)
    place = jnp.where(is_own, band + within, jnp.where(is_next, band + rows + within, within - band))
    code = (pc_ref[...] * STRIDE + place).astype(F32)
    strength = pw_ref[...].astype(F32) * pm_ref[...].astype(F32)
    meta[0:slots, :] = jnp.concatenate([code, code], axis=0).T
    meta[slots : 2 * slots, :] = jnp.concatenate([strength, strength], axis=0).T

    pl.semaphore_wait(barrier, cells - 1 + dirs - 1)

    def to_right(p):
        return pltpu.make_async_remote_copy(
            src_ref=send.at[p, band : 2 * band + rows, :],
            dst_ref=from_prev.at[p],
            send_sem=ssem.at[0, p],
            recv_sem=rsem.at[0, p],
            device_id=(right, my_dir),
            device_id_type=pl.DeviceIdType.MESH,
        )

    def to_left(p):
        return pltpu.make_async_remote_copy(
            src_ref=send.at[p, 0 : band + rows, :],
            dst_ref=from_next.at[p],
            send_sem=ssem.at[1, p],
            recv_sem=rsem.at[1, p],
            device_id=(left, my_dir),
            device_id_type=pl.DeviceIdType.MESH,
        )

    def meta_copy(i, dst, who):
        return pltpu.make_async_remote_copy(
            src_ref=meta,
            dst_ref=dst,
            send_sem=msem.at[i],
            recv_sem=mrsem.at[i],
            device_id=(who, my_dir),
            device_id_type=pl.DeviceIdType.MESH,
        )

    meta_right = meta_copy(0, meta_prev, right)
    meta_left = meta_copy(1, meta_next, left)
    meta_right.start()
    meta_left.start()
    for p in range(pairs):
        to_right(p).start()
        to_left(p).start()

    gap = STRIDE - order

    def place_class(k, c):
        te[k] = jnp.zeros((STRIDE, STRIDE), BF16)
        te[k, 0:order, 0:order] = tr_ref[k]
        full = te[k].astype(F32)
        to[k] = pltpu.roll(pltpu.roll(full, gap, 0), gap, 1).astype(BF16)
        turned = full.T
        tet[k] = turned.astype(BF16)
        tot[k] = pltpu.roll(pltpu.roll(turned, gap, 0), gap, 1).astype(BF16)
        return c

    lax.fori_loop(0, classes, place_class, 0)

    extent = rows + 2 * band
    step = 16
    lane = lax.broadcasted_iota(jnp.int32, (step, extent), 1).astype(F32)
    for b in range(rows // step):
        at = b * step
        cb = [jnp.broadcast_to(code[at : at + step, m : m + 1], (step, extent)) - lane for m in range(slots)]
        sb = [jnp.broadcast_to(strength[at : at + step, m : m + 1], (step, extent)) for m in range(slots)]
        for k in range(classes):
            acc = jnp.zeros((step, extent), F32)
            for m in range(slots):
                acc = acc + jnp.where(cb[m] == F32(k * STRIDE), sb[m], F32(0.0))
            pick[k * rows + at : k * rows + at + step, :] = acc.astype(BF16)

    meta_right.wait_recv()
    meta_left.wait_recv()
    low = lax.broadcasted_iota(jnp.int32, (slots, extent), 1) < rows
    code_a = jnp.where(low, meta_prev[0:slots, :] - F32(band + rows), meta[0:slots, :] - F32(band))
    str_a = jnp.where(low, meta_prev[slots : 2 * slots, :], meta[slots : 2 * slots, :])
    code_b = meta_next[0:slots, :] + F32(band)
    str_b = meta_next[slots : 2 * slots, :]
    for b in range(rows // step):
        at = b * step
        sub = lax.broadcasted_iota(jnp.int32, (step, extent), 0).astype(F32) + F32(at)
        for cc, ss, lo_lane, width in ((code_a, str_a, 0, extent), (code_b, str_b, extent, rows)):
            cb = [jnp.broadcast_to(cc[m : m + 1, :], (step, extent)) - sub for m in range(slots)]
            for k in range(classes):
                acc = jnp.zeros((step, extent), F32)
                for m in range(slots):
                    sm = jnp.broadcast_to(ss[m : m + 1, :], (step, extent))
                    acc = acc + jnp.where(cb[m] == F32(k * STRIDE), sm, F32(0.0))
                dpick[k * rows + at : k * rows + at + step, lo_lane : lo_lane + width] = acc[:, :width].astype(BF16)

    sums = [jnp.zeros((8, 128), F32) for _ in range(4)]
    for p in range(pairs):
        to_right(p).wait_recv()
        to_left(p).wait_recv()
        around = jnp.concatenate(
            [from_prev[p, rows:, :], send[p, 0:band, :], send[p, band + rows :, :], from_next[p, 0:band, :]], axis=0
        )
        gs[...] = jnp.dot(pick[...], around, preferred_element_type=F32).astype(BF16)
        spread = jnp.concatenate(
            [from_prev[p, 0:rows, :], send[p, band : band + rows, :], from_next[p, band:, :]], axis=0
        )
        whole = jnp.dot(dpick[...], spread, preferred_element_type=F32)
        hi = whole.astype(BF16)
        ghi[...] = hi
        glo[...] = (whole - hi.astype(F32)).astype(BF16)
        even = jnp.zeros((rows, STRIDE), F32)
        odd = jnp.zeros((rows, STRIDE), F32)
        deven = jnp.zeros((2 * rows, STRIDE), F32)
        dodd = jnp.zeros((2 * rows, STRIDE), F32)
        skip = wide - STRIDE
        for k in range(classes):
            r = slice(k * rows, (k + 1) * rows)
            even = even + jnp.dot(gs[r, 0:STRIDE], te[k], preferred_element_type=F32)
            odd = odd + jnp.dot(gs[r, skip:], to[k], preferred_element_type=F32)
            both = jnp.concatenate([ghi[r, :], glo[r, :]], axis=0)
            deven = deven + jnp.dot(both[:, 0:STRIDE], tet[k], preferred_element_type=F32)
            dodd = dodd + jnp.dot(both[:, skip:], tot[k], preferred_element_type=F32)
        de = deven[:rows] + deven[rows:]
        do = dodd[:rows] + dodd[rows:]
        mid = STRIDE - skip
        coupled = jnp.concatenate([even[:, :skip], even[:, skip:] + odd[:, :mid], odd[:, mid:]], axis=1)
        back = jnp.concatenate([de[:, :skip], de[:, skip:] + do[:, :mid], do[:, mid:]], axis=1)
        x = inc_ref[:, p * wide : (p + 1) * wide]
        image = x - gain[...] * coupled
        dual = x - back
        img_ref[:, p * wide : (p + 1) * wide] = image
        dual_ref[:, p * wide : (p + 1) * wide] = dual
        sums[0] = sums[0] + folded(x * x)
        sums[1] = sums[1] + folded(x * image)
        sums[2] = sums[2] + folded(x * dual)
        sums[3] = sums[3] + folded(image * dual)

    mine = jnp.concatenate(
        [jnp.sum(s, axis=0, keepdims=True) for s in sums] + [jnp.zeros((4, 128), F32)], axis=0
    )
    red_d[my_dir] = mine

    def dir_copy(t, slot):
        return pltpu.make_async_remote_copy(
            src_ref=red_d.at[slot],
            dst_ref=red_d.at[slot],
            send_sem=dssem.at[t],
            recv_sem=drsem.at[slot],
            device_id=(me, lax.rem(my_dir + t, dirs)),
            device_id_type=pl.DeviceIdType.MESH,
        )

    def cell_copy(t, slot):
        return pltpu.make_async_remote_copy(
            src_ref=red_c.at[slot],
            dst_ref=red_c.at[slot],
            send_sem=cssem.at[t],
            recv_sem=crsem.at[slot],
            device_id=(lax.rem(me + t, cells), my_dir),
            device_id_type=pl.DeviceIdType.MESH,
        )

    for t in range(1, dirs):
        dir_copy(t, my_dir).start()
    for t in range(1, dirs):
        dir_copy(t, lax.rem(my_dir + t, dirs)).wait_recv()
    red_c[me] = jnp.sum(red_d[...], axis=0)

    def cell_start(t, c):
        cell_copy(t, me).start()
        return c

    def cell_wait(t, c):
        cell_copy(t, lax.rem(me + t, cells)).wait_recv()
        return c

    lax.fori_loop(1, cells, cell_start, 0)
    lax.fori_loop(1, cells, cell_wait, 0)
    total = jnp.sum(jnp.sum(red_c[...], axis=0), axis=1, keepdims=True)
    norm_old = total[0:1]
    along_image = total[1:2]
    along_dual = total[2:3]
    cross = total[3:4]
    size = norm_old / along_image
    norm_new = norm_old - size * (along_image + along_dual) + size * size * cross
    ratio = norm_new / norm_old
    coef_ref[0:1, :] = jnp.broadcast_to(size, (1, 128))
    coef_ref[1:2, :] = jnp.broadcast_to(ratio, (1, 128))
    coef_ref[2:8, :] = jnp.zeros((6, 128), F32)

    meta_right.wait_send()
    meta_left.wait_send()
    for p in range(pairs):
        to_right(p).wait_send()
        to_left(p).wait_send()
    for t in range(1, dirs):
        dir_copy(t, my_dir).wait_send()

    def cell_sent(t, c):
        cell_copy(t, me).wait_send()
        return c

    lax.fori_loop(1, cells, cell_sent, 0)


def on_device(cells, dirs, incident, scattering, translations, pair_sphere, pair_class, pair_weight, pair_mask):
    rows, columns = incident.shape
    classes, order, _ = translations.shape
    slots = pair_sphere.shape[1]
    wide = 2 * order
    pairs = columns // wide
    vmem = pl.BlockSpec(memory_space=pltpu.VMEM)
    image, dual_image, coef = pl.pallas_call(
        functools.partial(kernel, cells, dirs),
        out_shape=(
            jax.ShapeDtypeStruct((rows, columns), F32),
            jax.ShapeDtypeStruct((rows, columns), F32),
            jax.ShapeDtypeStruct((8, 128), F32),
        ),
        in_specs=[vmem] * 7,
        out_specs=(vmem, vmem, vmem),
        scratch_shapes=[
            pltpu.VMEM((pairs, 2 * rows, wide), BF16),
            pltpu.VMEM((pairs, 3 * rows // 2, wide), BF16),
            pltpu.VMEM((pairs, 3 * rows // 2, wide), BF16),
            pltpu.VMEM((2 * slots, 2 * rows), F32),
            pltpu.VMEM((2 * slots, 2 * rows), F32),
            pltpu.VMEM((2 * slots, 2 * rows), F32),
            pltpu.VMEM((rows, wide), F32),
            pltpu.VMEM((classes * rows, 2 * rows), BF16),
            pltpu.VMEM((classes * rows, 3 * rows), BF16),
            pltpu.VMEM((classes, STRIDE, STRIDE), BF16),
            pltpu.VMEM((classes, STRIDE, STRIDE), BF16),
            pltpu.VMEM((classes, STRIDE, STRIDE), BF16),
            pltpu.VMEM((classes, STRIDE, STRIDE), BF16),
            pltpu.VMEM((classes * rows, wide), BF16),
            pltpu.VMEM((classes * rows, wide), BF16),
            pltpu.VMEM((classes * rows, wide), BF16),
            pltpu.VMEM((dirs, 8, 128), F32),
            pltpu.VMEM((cells, 8, 128), F32),
            pltpu.SemaphoreType.DMA((2, pairs)),
            pltpu.SemaphoreType.DMA((2, pairs)),
            pltpu.SemaphoreType.DMA((2,)),
            pltpu.SemaphoreType.DMA((2,)),
            pltpu.SemaphoreType.DMA((dirs,)),
            pltpu.SemaphoreType.DMA((dirs,)),
            pltpu.SemaphoreType.DMA((cells,)),
            pltpu.SemaphoreType.DMA((cells,)),
        ],
        compiler_params=pltpu.CompilerParams(
            collective_id=0, has_side_effects=True, vmem_limit_bytes=32 * 1024 * 1024
        ),
    )(incident, scattering, translations, pair_sphere, pair_class, pair_weight, pair_mask)
    size = coef[0, 0]
    ratio = coef[1, 0]
    residual = incident - size * image
    return (size * incident, residual, incident - size * dual_image, residual + ratio * incident)


def solution(mesh):
    cells, dirs = mesh.shape["cells"], mesh.shape["dirs"]
    split = P("cells", "dirs")
    by_cell = P("cells", None)
    return jax.shard_map(
        functools.partial(on_device, cells, dirs),
        mesh=mesh,
        in_specs=(split, by_cell, P(), by_cell, by_cell, by_cell, by_cell),
        out_specs=(split, split, split, split),
        check_vma=False,
    )
```

time: 117 us -> 36.3 us (0.31)
  blocking collectives: 40.4 us -> 0 us
  matrix products: 37 us -> 0 us
  Pallas kernels: 0 us -> 28.5 us
  local copies, waits for them, and re-layouts: 15.6 us -> 4.37 us
  starting transfers between devices: 10.8 us -> 0 us
  between operations: 5.4 us -> 0.69 us
  other arithmetic: 5.37 us -> 2.49 us
    psum x1 -> x0, blocking collectives: 40.4 us -> none  [on_device(): lax.psum((jnp.sum(incident * incident), jnp.sum(incident * image), jnp.su...]
    dot_general x33 -> x0, matrix products: 37 us -> none  [the longest x8 10.7 us: dual_step(): lax.dot_general(block, moved.reshape(spheres, columns), (((0,), (0,)), ((...]
    pallas_call x0 -> x1, Pallas kernels: none -> 28.5 us  [on_device(): pl.pallas_call(functools.partial(kernel, cells, dirs), out_shape=(jax.Sha...]
    ppermute x4 -> x0, starting transfers between devices: 10.8 us -> none  [the longest x1 6.06 us: extended(): after = lax.ppermute(leading, axis, down)]
    while x32 -> x0, local copies, waits for them, and re-layouts: 5.76 us -> none
    reshape x25 -> x0, local copies, waits for them, and re-layouts: 4.83 us -> none  [the longest x8 1.81 us: primal_step(): summed.reshape(spheres * groups, order)]
    unnamed x14 -> x16, local copies, waits for them, and re-layouts: 0.87 us -> 3.78 us
    sub x0 -> x1, other arithmetic: none -> 2.49 us  [on_device(): incident - size * dual_image]
  transfers between devices with their start and end apart: 4 -> 0, of which waited for: 0 -> 0; matrix products, arithmetic and copies ran while one was open for 41% -> 0% of each run, Pallas kernels for 0% -> 0%
where the time goes in v1:
time: 36.3 us; the launch traced here: 36 us
  Pallas kernels  28.5 us (79%)
  local copies, waits for them, and re-layouts  4.37 us (12%)
  other arithmetic  2.49 us (7%)
  between operations  0.69 us (2%)
    pallas_call x1, Pallas kernels, on_device(): pl.pallas_call(functools.partial(kernel, cells, dirs), out_shape=(jax.Sha...  28.5 us
    unnamed x16, local copies, waits for them, and re-layouts  3.78 us
    sub x1, other arithmetic, on_device(): incident - size * dual_image  2.49 us

profile of v1, /device:TPU:0, one launch (start us, length us, event | category | flops | bytes accessed | tf_op | source)
XLA Modules:
  0.0 36.0 jit_solution(8143428240517899122)
XLA Ops:
  0.6 0.0 copy-start.3
  0.6 0.0 copy-start.4
  0.7 0.8 %copy.13.pw_ref = bf16[64,16]{1,0:T(8,128)(2,1)S(1)} copy(bf16[64,16]{0,1:T(8,128)(2,1)} %param.12) | data formatting | bytes 4096 | tf_op args[5]
  1.4 0.0 copy-done.3
  1.4 0.0 copy-start.2
  1.5 0.1 copy.11.ps_ref
  1.5 0.0 copy-done.4
  1.5 0.0 copy-start.5
  1.6 0.1 copy.12.pc_ref
  1.6 0.6 %copy-done.5 = s32[64,16]{0,1:T(8,128)S(1)} copy-done((s32[64,16]{0,1:T(8,128)S(1)}, s32[64,16]{0,1:T(8,128)}, u32[]{:S(2)}) %copy-start.5) | copy-done | bytes 4120
  2.2 0.1 copy.14.pm_ref
  2.3 0.0 copy-done.2
  2.3 0.0 copy-start
  2.3 1.0 %copy-done = f32[64,1536]{1,0:T(8,128)S(1)} copy-done((f32[64,1536]{1,0:T(8,128)S(1)}, f32[64,1536]{1,0:T(8,128)}, u32[]{:S(2)}) %copy-start) | copy-done | bytes 393240
  3.3 0.0 copy-start.1
  3.3 1.1 %copy-done.1 = bf16[8,192,192]{2,1,0:T(8,128)(2,1)S(1)} copy-done((bf16[8,192,192]{2,1,0:T(8,128)(2,1)S(1)}, bf16[8,192,192]{2,1,0:T(8,128)(2,1)}, u32[]{:S(2)}) %copy-start.1) | copy-done | bytes 589848
  4.5 28.5 %shard_map.102 = (f32[64,1536]{1,0:T(8,128)S(1)}, f32[64,1536]{1,0:T(8,128)S(1)}, f32[8,128]{1,0:T(8,128)S(1)}) custom-call(f32[64,1536]{1,0:T(8,128)S(1)} %copy-done, f32[64,192]{1,0:T(8,128)S(1)} %copy-done.2, bf16[8,192,192]{2,1,0:T(8,128)(2,1)S(1)} %copy-done.1, s32[64,16]{1,0:T(8,128)S(1)} %copy.11.ps_ref, s32[64,16]{1,0:T(8,128)S(1)} %copy.12.pc_ref, ...), custom_call_target="tpu_custom_call" | custom-call | tf_op jit(solution)/shard_map/pallas_call | solution.py:316
  32.9 0.6 %fusion = (f32[1,1]{1,0:T(1,128)}, f32[1,1]{1,0:T(1,128)}) fusion(f32[8,128]{1,0:T(8,128)S(1)} %get-tuple-element.7), kind=kLoop, calls=%fused_computation.4 | loop fusion | bytes 16 | tf_op jit(solution)/shard_map/slice | solution.py:358
  33.5 2.5 %multiply_subtract_fusion = (f32[64,1536]{1,0:T(8,128)}, f32[64,1536]{1,0:T(8,128)}, f32[64,1536]{1,0:T(8,128)}, f32[64,1536]{1,0:T(8,128)}) fusion(f32[64,1536]{1,0:T(8,128)S(1)} %copy-done, f32[64,1536]{1,0:T(8,128)S(1)} %get-tuple-element.9, f32[]{:T(128)} %bitcast, f32[]{:T(128)} %bitcast.1, f32[64,1536]{1,0:T(8,128)S(1)} %get-tuple-element.8), kind=kLoop, calls=%fused_computation.1 | loop fusion | flops 688128 | bytes 2752520 | tf_op jit(solution)/shard_map/sub | solution.py:360
Async XLA Ops:
  0.6 0.8 %copy-start.3 = (s32[64,16]{0,1:T(8,128)S(1)}, s32[64,16]{0,1:T(8,128)}, u32[]{:S(2)}) copy-start(s32[64,16]{0,1:T(8,128)} %param.10) | copy-start | bytes 12292
  0.6 0.9 %copy-start.4 = (s32[64,16]{0,1:T(8,128)S(1)}, s32[64,16]{0,1:T(8,128)}, u32[]{:S(2)}) copy-start(s32[64,16]{0,1:T(8,128)} %param.11) | copy-start | bytes 12292
  1.4 0.9 %copy-start.2 = (f32[64,192]{1,0:T(8,128)S(1)}, f32[64,192]{1,0:T(8,128)}, u32[]{:S(2)}) copy-start(f32[64,192]{1,0:T(8,128)} %sc_ref.1) | copy-start | bytes 147460
  1.5 0.7 %copy-start.5 = (s32[64,16]{0,1:T(8,128)S(1)}, s32[64,16]{0,1:T(8,128)}, u32[]{:S(2)}) copy-start(s32[64,16]{0,1:T(8,128)} %param.13) | copy-start | bytes 12292
  2.3 1.0 %copy-start = (f32[64,1536]{1,0:T(8,128)S(1)}, f32[64,1536]{1,0:T(8,128)}, u32[]{:S(2)}) copy-start(f32[64,1536]{1,0:T(8,128)} %inc_ref.1) | copy-start | bytes 1179652
  3.3 1.1 %copy-start.1 = (bf16[8,192,192]{2,1,0:T(8,128)(2,1)S(1)}, bf16[8,192,192]{2,1,0:T(8,128)(2,1)}, u32[]{:S(2)}) copy-start(bf16[8,192,192]{2,1,0:T(8,128)(2,1)} %tr_ref.1) | copy-start | bytes 1769476

commit v2 on v1

v2 whole, which is shorter than its diff:
```python
import functools
import jax
import jax.numpy as jnp
from jax import lax
from jax.experimental import pallas as pl
from jax.experimental.pallas import tpu as pltpu
from jax.sharding import PartitionSpec as P

F32 = jnp.float32
BF16 = jnp.bfloat16
STRIDE = 256


def folded(x):
    rows, width = x.shape
    y = jnp.sum(x.reshape(rows // 8, 8, width), axis=0)
    out = y[:, :128]
    for at in range(128, width, 128):
        out = out + y[:, at : at + 128]
    return out


def kernel(
    cells,
    dirs,
    inc_hbm,
    sc_hbm,
    tr_hbm,
    ps_hbm,
    pc_hbm,
    pw_hbm,
    pm_hbm,
    img_hbm,
    dual_hbm,
    coef_ref,
    inc_ref,
    img_ref,
    dual_ref,
    sc_ref,
    tr_ref,
    ps_ref,
    pc_ref,
    pw_ref,
    pm_ref,
    send,
    near,
    far,
    meta,
    meta_near,
    meta_far,
    gain,
    pick,
    dpick,
    te,
    to,
    tet,
    tot,
    gs,
    ghi,
    glo,
    red,
    isem,
    osem,
    lsem,
    ssem,
    rsem,
    msem,
    mrsem,
    fssem,
    frsem,
    tssem,
    trsem,
):
    rows, columns = inc_ref.shape
    band = rows // 2
    classes, order, _ = tr_ref.shape
    slots = ps_ref.shape[0]
    wide = 2 * order
    pairs = columns // wide
    me = lax.axis_index("cells")
    my_dir = lax.axis_index("dirs")
    devices = cells * dirs
    here = me * dirs + my_dir
    odd_cell = lax.rem(me, 2)
    partner = me + 1 - 2 * odd_cell
    across = lax.rem(me - 1 + 2 * odd_cell + cells, cells)
    onward = lax.rem(me + 2 - 4 * odd_cell + cells, cells)

    def peer(t):
        other = lax.rem(here + t, devices)
        return (other // dirs, lax.rem(other, dirs)), other

    small = [
        pltpu.make_async_copy(a, b, lsem.at[i])
        for i, (a, b) in enumerate(
            (
                (sc_hbm, sc_ref),
                (ps_hbm, ps_ref),
                (pc_hbm, pc_ref),
                (pw_hbm, pw_ref),
                (pm_hbm, pm_ref),
                (tr_hbm, tr_ref),
            )
        )
    ]

    def incident_in(p):
        cut = (slice(None), slice(p * wide, (p + 1) * wide))
        return pltpu.make_async_copy(inc_hbm.at[cut], inc_ref.at[cut], isem.at[p])

    def results_out(p):
        cut = (slice(None), slice(p * wide, (p + 1) * wide))
        return (
            pltpu.make_async_copy(img_ref.at[cut], img_hbm.at[cut], osem.at[0, p]),
            pltpu.make_async_copy(dual_ref.at[cut], dual_hbm.at[cut], osem.at[1, p]),
        )

    barrier = pltpu.get_barrier_semaphore()

    def greet(t, c):
        pl.semaphore_signal(barrier, inc=1, device_id=peer(t)[0], device_id_type=pl.DeviceIdType.MESH)
        return c

    lax.fori_loop(1, devices, greet, 0)
    for copy in small[:5]:
        copy.start()
    for p in range(pairs):
        incident_in(p).start()
    small[5].start()

    for copy in small[1:5]:
        copy.wait()
    ps = ps_ref[...]
    owner = ps // rows
    within = ps - owner * rows
    is_own = owner == me
    is_near = owner == partner
    code = (
        pc_ref[...] * STRIDE + jnp.where(is_near, within, jnp.where(is_own, rows + within, 2 * rows + within))
    ).astype(F32)
    place = jnp.where(
        is_near,
        within - band * odd_cell,
        jnp.where(is_own, band + within, rows + band + within - band * (1 - odd_cell)),
    )
    column = (pc_ref[...] * STRIDE + place).astype(F32)
    strength = pw_ref[...].astype(F32) * pm_ref[...].astype(F32)
    meta[0:slots, :] = jnp.concatenate([code, code], axis=1)
    meta[slots : 2 * slots, :] = jnp.concatenate([strength, strength], axis=1)

    small[0].wait()
    gain[:, 0:order] = sc_ref[...]
    gain[:, order:wide] = sc_ref[...]
    g = gain[...]

    def fill(p):
        incident_in(p).wait()
        x = inc_ref[:, p * wide : (p + 1) * wide]
        src = x.astype(BF16)
        send[p, 0:band, :] = src[0:band]
        send[p, band : band + rows, :] = (g * x).astype(BF16)
        send[p, band + rows :, :] = src[band:]

    fill(0)
    pl.semaphore_wait(barrier, devices - 1)

    def to_partner(p):
        return pltpu.make_async_remote_copy(
            src_ref=send.at[p],
            dst_ref=near.at[p],
            send_sem=ssem.at[p],
            recv_sem=rsem.at[p],
            device_id=(partner, my_dir),
            device_id_type=pl.DeviceIdType.MESH,
        )

    pass_on = pl.multiple_of(band * (1 - odd_cell), band)

    def forward(p):
        return pltpu.make_async_remote_copy(
            src_ref=near.at[p, pl.ds(pass_on, band + rows), :],
            dst_ref=far.at[p],
            send_sem=fssem.at[p],
            recv_sem=frsem.at[p],
            device_id=(onward, my_dir),
            device_id_type=pl.DeviceIdType.MESH,
        )

    def meta_copy(i, dst, who):
        return pltpu.make_async_remote_copy(
            src_ref=meta,
            dst_ref=dst,
            send_sem=msem.at[i],
            recv_sem=mrsem.at[i],
            device_id=(who, my_dir),
            device_id_type=pl.DeviceIdType.MESH,
        )

    meta_a = meta_copy(0, meta_near, partner)
    meta_b = meta_copy(1, meta_far, across)
    meta_b.start()
    meta_a.start()
    for p in range(pairs):
        if p > 0:
            fill(p)
        to_partner(p).start()

    both = jnp.concatenate([column, strength], axis=0)
    both = jnp.concatenate([both, both], axis=1)
    flat = jnp.concatenate([both] * (128 // (2 * slots)), axis=0).T
    code = flat[0:rows, 0:slots]
    strength = flat[0:rows, slots : 2 * slots]
    small[5].wait()

    gap = STRIDE - order

    def place_class(k, c):
        te[k] = jnp.zeros((STRIDE, STRIDE), BF16)
        te[k, 0:order, 0:order] = tr_ref[k]
        full = te[k].astype(F32)
        to[k] = pltpu.roll(pltpu.roll(full, gap, 0), gap, 1).astype(BF16)
        turned = full.T
        tet[k] = turned.astype(BF16)
        tot[k] = pltpu.roll(pltpu.roll(turned, gap, 0), gap, 1).astype(BF16)
        return c

    lax.fori_loop(0, classes, place_class, 0)

    extent = rows + 2 * band
    step = 16
    lane = lax.broadcasted_iota(jnp.int32, (step, extent), 1).astype(F32)
    for b in range(rows // step):
        at = b * step
        cb = [jnp.broadcast_to(code[at : at + step, m : m + 1], (step, extent)) - lane for m in range(slots)]
        sb = [jnp.broadcast_to(strength[at : at + step, m : m + 1], (step, extent)) for m in range(slots)]
        for k in range(classes):
            acc = jnp.zeros((step, extent), F32)
            for m in range(slots):
                acc = acc + jnp.where(cb[m] == F32(k * STRIDE), sb[m], F32(0.0))
            pick[k * rows + at : k * rows + at + step, :] = acc.astype(BF16)

    meta_a.wait_recv()
    meta_b.wait_recv()
    low = lax.broadcasted_iota(jnp.int32, (slots, extent), 1) < rows
    code_a = jnp.where(low, meta_near[0:slots, :], meta[0:slots, :] - F32(rows))
    str_a = jnp.where(low, meta_near[slots : 2 * slots, :], meta[slots : 2 * slots, :])
    code_b = meta_far[0:slots, :] - F32(2 * rows)
    str_b = meta_far[slots : 2 * slots, :]
    for b in range(rows // step):
        at = b * step
        sub = lax.broadcasted_iota(jnp.int32, (step, extent), 0).astype(F32) + F32(at)
        for cc, ss, lo_lane, width in ((code_a, str_a, 0, extent), (code_b, str_b, extent, rows)):
            cb = [jnp.broadcast_to(cc[m : m + 1, :], (step, extent)) - sub for m in range(slots)]
            for k in range(classes):
                acc = jnp.zeros((step, extent), F32)
                for m in range(slots):
                    sm = jnp.broadcast_to(ss[m : m + 1, :], (step, extent))
                    acc = acc + jnp.where(cb[m] == F32(k * STRIDE), sm, F32(0.0))
                dpick[k * rows + at : k * rows + at + step, lo_lane : lo_lane + width] = acc[:, :width].astype(BF16)

    sums = [jnp.zeros((8, 128), F32) for _ in range(4)]
    near_band = pl.multiple_of((band + rows) * odd_cell, band)
    far_band = pl.multiple_of(rows * (1 - odd_cell), band)
    far_rows = pl.multiple_of(band * odd_cell, band)
    to_partner(0).wait_recv()
    forward(0).start()
    for p in range(pairs):
        if p + 1 < pairs:
            to_partner(p + 1).wait_recv()
            forward(p + 1).start()
        forward(p).wait_recv()
        around = jnp.concatenate(
            [
                near[p, pl.ds(near_band, band), :],
                send[p, 0:band, :],
                send[p, band + rows :, :],
                far[p, pl.ds(far_band, band), :],
            ],
            axis=0,
        )
        gs[...] = jnp.dot(pick[...], around, preferred_element_type=F32).astype(BF16)
        spread = jnp.concatenate(
            [near[p, band : band + rows, :], send[p, band : band + rows, :], far[p, pl.ds(far_rows, rows), :]], axis=0
        )
        whole = jnp.dot(dpick[...], spread, preferred_element_type=F32)
        hi = whole.astype(BF16)
        ghi[...] = hi
        glo[...] = (whole - hi.astype(F32)).astype(BF16)
        even = jnp.zeros((rows, STRIDE), F32)
        odd = jnp.zeros((rows, STRIDE), F32)
        deven = jnp.zeros((2 * rows, STRIDE), F32)
        dodd = jnp.zeros((2 * rows, STRIDE), F32)
        skip = wide - STRIDE
        for k in range(classes):
            r = slice(k * rows, (k + 1) * rows)
            even = even + jnp.dot(gs[r, 0:STRIDE], te[k], preferred_element_type=F32)
            odd = odd + jnp.dot(gs[r, skip:], to[k], preferred_element_type=F32)
            both = jnp.concatenate([ghi[r, :], glo[r, :]], axis=0)
            deven = deven + jnp.dot(both[:, 0:STRIDE], tet[k], preferred_element_type=F32)
            dodd = dodd + jnp.dot(both[:, skip:], tot[k], preferred_element_type=F32)
        de = deven[:rows] + deven[rows:]
        do = dodd[:rows] + dodd[rows:]
        mid = STRIDE - skip
        coupled = jnp.concatenate([even[:, :skip], even[:, skip:] + odd[:, :mid], odd[:, mid:]], axis=1)
        back = jnp.concatenate([de[:, :skip], de[:, skip:] + do[:, :mid], do[:, mid:]], axis=1)
        x = inc_ref[:, p * wide : (p + 1) * wide]
        image = x - gain[...] * coupled
        dual = x - back
        img_ref[:, p * wide : (p + 1) * wide] = image
        dual_ref[:, p * wide : (p + 1) * wide] = dual
        for copy in results_out(p):
            copy.start()
        sums[0] = sums[0] + folded(x * x)
        sums[1] = sums[1] + folded(x * image)
        sums[2] = sums[2] + folded(x * dual)
        sums[3] = sums[3] + folded(image * dual)

    mine = jnp.concatenate(
        [jnp.sum(s, axis=0, keepdims=True) for s in sums] + [jnp.zeros((4, 128), F32)], axis=0
    )
    red[here] = mine

    def sums_copy(t, slot):
        return pltpu.make_async_remote_copy(
            src_ref=red.at[slot],
            dst_ref=red.at[slot],
            send_sem=tssem.at[t],
            recv_sem=trsem.at[slot],
            device_id=peer(t)[0],
            device_id_type=pl.DeviceIdType.MESH,
        )

    def sums_start(t, c):
        sums_copy(t, here).start()
        return c

    def sums_wait(t, c):
        sums_copy(t, peer(t)[1]).wait_recv()
        return c

    lax.fori_loop(1, devices, sums_start, 0)
    lax.fori_loop(1, devices, sums_wait, 0)
    total = jnp.sum(jnp.sum(red[...], axis=0), axis=1, keepdims=True)
    norm_old = total[0:1]
    along_image = total[1:2]
    along_dual = total[2:3]
    cross = total[3:4]
    size = norm_old / along_image
    norm_new = norm_old - size * (along_image + along_dual) + size * size * cross
    ratio = norm_new / norm_old
    coef_ref[0:1, :] = jnp.broadcast_to(size, (1, 128))
    coef_ref[1:2, :] = jnp.broadcast_to(ratio, (1, 128))
    coef_ref[2:8, :] = jnp.zeros((6, 128), F32)

    meta_a.wait_send()
    meta_b.wait_send()
    for p in range(pairs):
        to_partner(p).wait_send()
        forward(p).wait_send()
        for copy in results_out(p):
            copy.wait()

    def sums_sent(t, c):
        sums_copy(t, here).wait_send()
        return c

    lax.fori_loop(1, devices, sums_sent, 0)


def finish(inc_ref, img_ref, dual_ref, coef_ref, sol_hbm, res_hbm, dres_hbm, dir_hbm, held, sem):
    rows, columns = inc_ref.shape
    size = coef_ref[0:1, 0:1]
    ratio = coef_ref[1:2, 0:1]
    copies = []
    step = rows // 4
    for b in range(4):
        cut = (slice(b * step, (b + 1) * step), slice(None))
        x = inc_ref[cut]
        residual = x - size * img_ref[cut]
        values = (size * x, residual, x - size * dual_ref[cut], residual + ratio * x)
        for i, (value, out) in enumerate(zip(values, (sol_hbm, res_hbm, dres_hbm, dir_hbm))):
            held[(i,) + cut] = value
            copy = pltpu.make_async_copy(held.at[(i,) + cut], out.at[cut], sem.at[i, b])
            copy.start()
            copies.append(copy)
    for copy in copies:
        copy.wait()


def on_device(cells, dirs, incident, scattering, translations, pair_sphere, pair_class, pair_weight, pair_mask):
    rows, columns = incident.shape
    classes, order, _ = translations.shape
    slots = pair_sphere.shape[1]
    anywhere = pl.BlockSpec(memory_space=pltpu.HBM)
    field = jax.ShapeDtypeStruct((rows, columns), F32)
    wide = 2 * order
    pairs = columns // wide
    vmem = pl.BlockSpec(memory_space=pltpu.VMEM)
    held = pl.pallas_call(
        functools.partial(kernel, cells, dirs),
        out_shape=(field,) * 2 + (jax.ShapeDtypeStruct((8, 128), F32),),
        in_specs=[anywhere] * 7,
        out_specs=(anywhere, anywhere, vmem),
        scratch_shapes=[
            pltpu.VMEM((rows, columns), F32),
            pltpu.VMEM((rows, columns), F32),
            pltpu.VMEM((rows, columns), F32),
            pltpu.VMEM((rows, order), F32),
            pltpu.VMEM((classes, order, order), BF16),
            pltpu.VMEM((slots, rows), jnp.int32),
            pltpu.VMEM((slots, rows), jnp.int32),
            pltpu.VMEM((slots, rows), BF16),
            pltpu.VMEM((slots, rows), jnp.int32),
            pltpu.VMEM((pairs, 2 * rows, wide), BF16),
            pltpu.VMEM((pairs, 2 * rows, wide), BF16),
            pltpu.VMEM((pairs, 3 * rows // 2, wide), BF16),
            pltpu.VMEM((2 * slots, 2 * rows), F32),
            pltpu.VMEM((2 * slots, 2 * rows), F32),
            pltpu.VMEM((2 * slots, 2 * rows), F32),
            pltpu.VMEM((rows, wide), F32),
            pltpu.VMEM((classes * rows, 2 * rows), BF16),
            pltpu.VMEM((classes * rows, 3 * rows), BF16),
            pltpu.VMEM((classes, STRIDE, STRIDE), BF16),
            pltpu.VMEM((classes, STRIDE, STRIDE), BF16),
            pltpu.VMEM((classes, STRIDE, STRIDE), BF16),
            pltpu.VMEM((classes, STRIDE, STRIDE), BF16),
            pltpu.VMEM((classes * rows, wide), BF16),
            pltpu.VMEM((classes * rows, wide), BF16),
            pltpu.VMEM((classes * rows, wide), BF16),
            pltpu.VMEM((cells * dirs, 8, 128), F32),
            pltpu.SemaphoreType.DMA((pairs,)),
            pltpu.SemaphoreType.DMA((2, pairs)),
            pltpu.SemaphoreType.DMA((6,)),
            pltpu.SemaphoreType.DMA((pairs,)),
            pltpu.SemaphoreType.DMA((pairs,)),
            pltpu.SemaphoreType.DMA((2,)),
            pltpu.SemaphoreType.DMA((2,)),
            pltpu.SemaphoreType.DMA((pairs,)),
            pltpu.SemaphoreType.DMA((pairs,)),
            pltpu.SemaphoreType.DMA((cells * dirs,)),
            pltpu.SemaphoreType.DMA((cells * dirs,)),
        ],
        compiler_params=pltpu.CompilerParams(
            collective_id=0, has_side_effects=True, vmem_limit_bytes=56 * 1024 * 1024
        ),
    )(incident, scattering, translations, pair_sphere.T, pair_class.T, pair_weight.T, pair_mask.T)
    return pl.pallas_call(
        finish,
        out_shape=(field,) * 4,
        in_specs=[vmem] * 4,
        out_specs=(anywhere,) * 4,
        scratch_shapes=[pltpu.VMEM((4, rows, columns), F32), pltpu.SemaphoreType.DMA((4, 4))],
    )(incident, *held)


def solution(mesh):
    cells, dirs = mesh.shape["cells"], mesh.shape["dirs"]
    split = P("cells", "dirs")
    by_cell = P("cells", None)
    return jax.shard_map(
        functools.partial(on_device, cells, dirs),
        mesh=mesh,
        in_specs=(split, by_cell, P(), by_cell, by_cell, by_cell, by_cell),
        out_specs=(split, split, split, split),
        check_vma=False,
    )
```

time: 36.3 us -> 33.2 us (0.915)
  local copies, waits for them, and re-layouts: 4.37 us -> 0 us
  Pallas kernels: 28.5 us -> 32.4 us
  other arithmetic: 2.49 us -> 0 us
    pallas_call x1 -> x2, Pallas kernels: 28.5 us -> 32.4 us  [the longest x1 29.9 us: on_device(): pl.pallas_call(functools.partial(kernel, cells, dirs), out_shape=(field,)...]
    unnamed x16 -> x0, local copies, waits for them, and re-layouts: 3.78 us -> none
    sub x1 -> x0, other arithmetic: 2.49 us -> none  [on_device(): incident - size * dual_image]
    slice x1 -> x0, local copies, waits for them, and re-layouts: 0.59 us -> none  [on_device(): ratio = coef[1, 0]]
where the time goes in v2:
time: 33.2 us; the launch traced here: 33.1 us
  Pallas kernels  32.4 us (98%)
  between operations  0.64 us (2%)
    pallas_call x1, Pallas kernels, on_device(): pl.pallas_call(functools.partial(kernel, cells, dirs), out_shape=(field,)...  29.9 us
    pallas_call x1, Pallas kernels, on_device(): pl.pallas_call(finish, out_shape=(field,) * 4, in_specs=[vmem] * 4, out_s...  2.55 us

profile of v2, /device:TPU:0, one launch (start us, length us, event | category | flops | bytes accessed | tf_op | source)
XLA Modules:
  0.0 33.1 jit_solution(4918262369227486720)
XLA Ops:
  0.6 29.9 %shard_map.102 = (f32[64,1536]{1,0:T(8,128)}, f32[64,1536]{1,0:T(8,128)}, f32[8,128]{1,0:T(8,128)}) custom-call(f32[64,1536]{1,0:T(8,128)} %inc_ref.1, f32[64,192]{1,0:T(8,128)} %sc_hbm.1, bf16[8,192,192]{2,1,0:T(8,128)(2,1)} %tr_hbm.1, s32[16,64]{1,0:T(8,128)} %bitcast.4, s32[16,64]{1,0:T(8,128)} %bitcast.5, bf16[16,64]{1,0:T(8,128)(2,1)} %bitcast.7, ...), custom_call_target="tpu_custom_call" | custom-call | tf_op jit(solution)/shard_map/pallas_call | solution.py:399
  30.5 2.6 %shard_map.103 = (f32[64,1536]{1,0:T(8,128)}, f32[64,1536]{1,0:T(8,128)}, f32[64,1536]{1,0:T(8,128)}, f32[64,1536]{1,0:T(8,128)}) custom-call(f32[64,1536]{1,0:T(8,128)} %inc_ref.1, f32[64,1536]{1,0:T(8,128)} %get-tuple-element.7.img_ref, f32[64,1536]{1,0:T(8,128)} %get-tuple-element.8.dual_ref, f32[8,128]{1,0:T(8,128)} %get-tuple-element.9.coef_ref), custom_call_target="tpu_custom_call" | custom-call | tf_op jit(solution)/shard_map/pallas_call | solution.py:447

commit v3 on v2

--- a/solution.py
+++ b/solution.py
@@ -86,9 +86,10 @@
     across = lax.rem(me - 1 + 2 * odd_cell + cells, cells)
     onward = lax.rem(me + 2 - 4 * odd_cell + cells, cells)
 
-    def peer(t):
-        other = lax.rem(here + t, devices)
-        return (other // dirs, lax.rem(other, dirs)), other
+    def peer(t, d):
+        cell = me + t
+        side = my_dir + d
+        return (jnp.where(cell >= cells, cell - cells, cell), jnp.where(side >= dirs, side - dirs, side))
 
     small = [
         pltpu.make_async_copy(a, b, lsem.at[i])
@@ -117,16 +118,20 @@
 
     barrier = pltpu.get_barrier_semaphore()
 
-    def greet(t, c):
-        pl.semaphore_signal(barrier, inc=1, device_id=peer(t)[0], device_id_type=pl.DeviceIdType.MESH)
-        return c
-
-    lax.fori_loop(1, devices, greet, 0)
     for copy in small[:5]:
         copy.start()
     for p in range(pairs):
         incident_in(p).start()
     small[5].start()
+
+    def greet(t, c):
+        for d in range(dirs):
+            pl.semaphore_signal(barrier, inc=1, device_id=peer(t, d), device_id_type=pl.DeviceIdType.MESH)
+        return c
+
+    for d in range(1, dirs):
+        pl.semaphore_signal(barrier, inc=1, device_id=peer(0, d), device_id_type=pl.DeviceIdType.MESH)
+    lax.fori_loop(1, cells, greet, 0)
 
     for copy in small[1:5]:
         copy.wait()
@@ -226,6 +231,11 @@
 
     lax.fori_loop(0, classes, place_class, 0)
 
+    def receive(p):
+        to_partner(p).wait_recv()
+        forward(p).start()
+
+    receive(0)
     extent = rows + 2 * band
     step = 16
     lane = lax.broadcasted_iota(jnp.int32, (step, extent), 1).astype(F32)
@@ -239,6 +249,7 @@
                 acc = acc + jnp.where(cb[m] == F32(k * STRIDE), sb[m], F32(0.0))
             pick[k * rows + at : k * rows + at + step, :] = acc.astype(BF16)
 
+    receive(1)
     meta_a.wait_recv()
     meta_b.wait_recv()
     low = lax.broadcasted_iota(jnp.int32, (slots, extent), 1) < rows
@@ -262,12 +273,10 @@
     near_band = pl.multiple_of((band + rows) * odd_cell, band)
     far_band = pl.multiple_of(rows * (1 - odd_cell), band)
     far_rows = pl.multiple_of(band * odd_cell, band)
-    to_partner(0).wait_recv()
-    forward(0).start()
+    receive(2)
     for p in range(pairs):
-        if p + 1 < pairs:
-            to_partner(p + 1).wait_recv()
-            forward(p + 1).start()
+        if p + 3 < pairs:
+            receive(p + 3)
         forward(p).wait_recv()
         around = jnp.concatenate(
             [
@@ -320,26 +329,26 @@
     )
     red[here] = mine
 
-    def sums_copy(t, slot):
+    def sums_copy(t, d):
         return pltpu.make_async_remote_copy(
-            src_ref=red.at[slot],
-            dst_ref=red.at[slot],
-            send_sem=tssem.at[t],
-            recv_sem=trsem.at[slot],
-            device_id=peer(t)[0],
+            src_ref=red.at[here],
+            dst_ref=red.at[here],
+            send_sem=tssem,
+            recv_sem=trsem,
+            device_id=peer(t, d),
             device_id_type=pl.DeviceIdType.MESH,
         )
 
     def sums_start(t, c):
-        sums_copy(t, here).start()
+        for d in range(dirs):
+            sums_copy(t, d).start()
         return c
 
-    def sums_wait(t, c):
-        sums_copy(t, peer(t)[1]).wait_recv()
-        return c
-
-    lax.fori_loop(1, devices, sums_start, 0)
-    lax.fori_loop(1, devices, sums_wait, 0)
+    others = red.at[0 : devices - 1]
+    lax.fori_loop(1, cells, sums_start, 0)
+    for d in range(1, dirs):
+        sums_copy(0, d).start()
+    pltpu.make_async_copy(others, others, trsem).wait()
     total = jnp.sum(jnp.sum(red[...], axis=0), axis=1, keepdims=True)
     norm_old = total[0:1]
     along_image = total[1:2]
@@ -360,11 +369,7 @@
         for copy in results_out(p):
             copy.wait()
 
-    def sums_sent(t, c):
-        sums_copy(t, here).wait_send()
-        return c
-
-    lax.fori_loop(1, devices, sums_sent, 0)
+    pltpu.make_async_copy(others, others, tssem).wait()
 
 
 def finish(inc_ref, img_ref, dual_ref, coef_ref, sol_hbm, res_hbm, dres_hbm, dir_hbm, held, sem):
@@ -437,8 +442,8 @@
             pltpu.SemaphoreType.DMA((2,)),
             pltpu.SemaphoreType.DMA((pairs,)),
             pltpu.SemaphoreType.DMA((pairs,)),
-            pltpu.SemaphoreType.DMA((cells * dirs,)),
-            pltpu.SemaphoreType.DMA((cells * dirs,)),
+            pltpu.SemaphoreType.DMA,
+            pltpu.SemaphoreType.DMA,
         ],
         compiler_params=pltpu.CompilerParams(
             collective_id=0, has_side_effects=True, vmem_limit_bytes=56 * 1024 * 1024

time: 33.2 us -> 32 us (0.964)
  Pallas kernels: 32.4 us -> 31.2 us
    pallas_call x1, Pallas kernels: 29.9 us -> 28.7 us  [on_device(): pl.pallas_call(functools.partial(kernel, cells, dirs), out_shape=(field,)...]
where the time goes in v3:
time: 32 us; the launch traced here: 31.9 us
  Pallas kernels  31.2 us (98%)
  between operations  0.64 us (2%)
    pallas_call x1, Pallas kernels, on_device(): pl.pallas_call(functools.partial(kernel, cells, dirs), out_shape=(field,)...  28.7 us
    pallas_call x1, Pallas kernels, on_device(): pl.pallas_call(finish, out_shape=(field,) * 4, in_specs=[vmem] * 4, out_s...  2.55 us

profile of v3, /device:TPU:0, one launch (start us, length us, event | category | flops | bytes accessed | tf_op | source)
XLA Modules:
  0.0 31.9 jit_solution(2506013708844865865)
XLA Ops:
  0.6 28.7 %shard_map.102 = (f32[64,1536]{1,0:T(8,128)}, f32[64,1536]{1,0:T(8,128)}, f32[8,128]{1,0:T(8,128)}) custom-call(f32[64,1536]{1,0:T(8,128)} %inc_ref.1, f32[64,192]{1,0:T(8,128)} %sc_hbm.1, bf16[8,192,192]{2,1,0:T(8,128)(2,1)} %tr_hbm.1, s32[16,64]{1,0:T(8,128)} %bitcast.4, s32[16,64]{1,0:T(8,128)} %bitcast.5, bf16[16,64]{1,0:T(8,128)(2,1)} %bitcast.7, ...), custom_call_target="tpu_custom_call" | custom-call | tf_op jit(solution)/shard_map/pallas_call | solution.py:404
  29.3 2.6 %shard_map.103 = (f32[64,1536]{1,0:T(8,128)}, f32[64,1536]{1,0:T(8,128)}, f32[64,1536]{1,0:T(8,128)}, f32[64,1536]{1,0:T(8,128)}) custom-call(f32[64,1536]{1,0:T(8,128)} %inc_ref.1, f32[64,1536]{1,0:T(8,128)} %get-tuple-element.7.img_ref, f32[64,1536]{1,0:T(8,128)} %get-tuple-element.8.dual_ref, f32[8,128]{1,0:T(8,128)} %get-tuple-element.9.coef_ref), custom_call_target="tpu_custom_call" | custom-call | tf_op jit(solution)/shard_map/pallas_call | solution.py:452
